TPU v7x, 32 devices: a whole 2x2x4 slice. The times are simulated.
32 devices in a mesh: gx: 2 (over core), gy: 4 (over y, x), af: 4 (over z).
Axes of the slice: x: 2, y: 2, z: 4, core: 2. Of those that a mesh axis runs over, the one named last changes fastest.
Arguments:
- features: bfloat16 [8192, 1024], P(('gx', 'gy'), 'af'), may hold values from -6 to 6
- adj_tiles: bfloat16 [64, 4, 128, 128], P(('gx', 'gy')), may hold values from -0.25 to 0.25
- col_block: int32 [64, 4], P(('gx', 'gy')), may hold values from 0 to 7, as said below
- send_rows: int32 [32, 384], P(('gx', 'gy')), may hold values from 0 to 1023
- send_counts: int32 [32], P(('gx', 'gy')), may hold values from 96 to 384, as said below
- recv_target: int32 [32, 384], P(('gx', 'gy')), may hold values from 0 to 1023
- edge_weight: float32 [32, 384], P(('gx', 'gy')), may hold values from -3 to 3
- labels: int32 [8192], P(('gx', 'gy')), may hold values from 0 to 127
- w_hidden: bfloat16 [1024, 1024], P('af'), may hold values from -0.1875 to 0.1875
- w_classes: bfloat16 [1024, 128], P('af'), may hold values from -0.5 to 0.5
Outputs:
- grad_w_hidden: float32 [1024, 1024], P('af')
- grad_w_classes: float32 [1024, 128], P('af')
Inputs may be any that keep to these rules, and one draw needn't show every extreme that they name: `send_counts`: entry 4 p + d is the number of leading live slots in row 4 p + d of send_rows; some entry equals 384. `col_block`: entry k = 0 of row t is t mod (8), the tile's own block; the 4 entries of a row are distinct. `send_rows`: rows of the sending partition; repeats possible. `recv_target`: rows of the receiving partition; repeats possible.
All inputs are finite; a program needn't handle non-finite values.
Results may differ from a plain program's by a relative error of at most 0.008.
Values may be sent and summed in bfloat16 or wider, within the bound.
A program may use at most 64 MiB of HBM per device.

v0:
```python
import jax
import jax.numpy as jnp
from jax import lax
from jax.sharding import PartitionSpec as P


def with_halo(block, sides, width):
    for axis, dim in sides:
        count = lax.axis_size(axis)
        forward = [(i, i + 1) for i in range(count - 1)]
        backward = [(target, source) for source, target in forward]
        low = lax.ppermute(
            lax.slice_in_dim(block, block.shape[dim] - width, None, axis=dim), axis, forward
        )
        high = lax.ppermute(lax.slice_in_dim(block, 0, width, axis=dim), axis, backward)
        block = jnp.concatenate([low, block, high], axis=dim)
    return block


def trade_rims(to_lower_x, to_upper_x, to_lower_y, to_upper_y):
    along_x = with_halo(jnp.stack([to_lower_x, to_upper_x]), (("gx", 0),), 1)
    along_y = with_halo(jnp.stack([to_lower_y, to_upper_y]), (("gy", 0),), 1)
    return (along_x[0], along_x[3], along_y[0], along_y[3])


def aggregate(node_field, graph_parts):
    adj_tiles, col_block, send_rows, slot_live, recv_target, edge_weight = graph_parts
    feat_width = node_field.shape[1]
    blocks = adj_tiles.shape[0]
    field_blocks = node_field.reshape(blocks, -1, feat_width)
    local_sum = jnp.zeros(field_blocks.shape, jnp.float32)
    for slot in range(adj_tiles.shape[1]):
        picked = field_blocks[col_block[:, slot]]
        local_sum = local_sum + jnp.einsum(
            "bij,bjf->bif", adj_tiles[:, slot], picked, preferred_element_type=jnp.float32
        )
    local_sum = local_sum.reshape(-1, feat_width)
    outgoing = jnp.where(
        slot_live[:, :, None], node_field[send_rows], jnp.zeros((), node_field.dtype)
    )
    arrived = jnp.stack(trade_rims(outgoing[1], outgoing[0], outgoing[3], outgoing[2]))
    weighted = edge_weight[:, :, None] * arrived.astype(jnp.float32)
    return local_sum.at[recv_target.reshape(-1)].add(weighted.reshape(-1, feat_width))


def aggregate_back(grad_field, graph_parts):
    adj_tiles, col_block, send_rows, slot_live, recv_target, edge_weight = graph_parts
    feat_width = grad_field.shape[1]
    blocks = adj_tiles.shape[0]
    grad_blocks = grad_field.reshape(blocks, -1, feat_width)
    local_sum = jnp.zeros(grad_blocks.shape, jnp.float32)
    for slot in range(adj_tiles.shape[1]):
        spread = jnp.einsum(
            "bij,bif->bjf", adj_tiles[:, slot], grad_blocks, preferred_element_type=jnp.float32
        )
        local_sum = local_sum.at[col_block[:, slot]].add(spread)
    local_sum = local_sum.reshape(-1, feat_width)
    back_terms = (edge_weight[:, :, None] * grad_field[recv_target].astype(jnp.float32)).astype(
        jnp.bfloat16
    )
    came_back = trade_rims(back_terms[0], back_terms[1], back_terms[2], back_terms[3])
    returned = jnp.stack([came_back[1], came_back[0], came_back[3], came_back[2]]).astype(
        jnp.float32
    )
    returned = jnp.where(slot_live[:, :, None], returned, jnp.zeros((), jnp.float32))
    return local_sum.at[send_rows.reshape(-1)].add(returned.reshape(-1, feat_width))


def local(
    features,
    adj_tiles,
    col_block,
    send_rows,
    send_counts,
    recv_target,
    edge_weight,
    labels,
    w_hidden,
    w_classes,
):
    slot_live = jnp.arange(send_rows.shape[1], dtype=jnp.int32)[None, :] < send_counts[:, None]
    graph_parts = (adj_tiles, col_block, send_rows, slot_live, recv_target, edge_weight)
    mixed_own = aggregate(features, graph_parts).astype(jnp.bfloat16)
    mixed_all = lax.all_gather(mixed_own, "af", axis=1, tiled=True)
    w_columns = lax.all_to_all(w_hidden, "af", split_axis=1, concat_axis=0, tiled=True)
    pre_act = jnp.dot(mixed_all, w_columns, preferred_element_type=jnp.float32)
    hidden = jax.nn.silu(pre_act).astype(jnp.bfloat16)
    mixed_hidden = aggregate(hidden, graph_parts).astype(jnp.bfloat16)
    logits = lax.psum(jnp.dot(mixed_hidden, w_classes, preferred_element_type=jnp.float32), "af")
    exponent = jnp.exp(logits - jnp.max(logits, axis=1, keepdims=True))
    probability = exponent / jnp.sum(exponent, axis=1, keepdims=True)
    onehot = (labels[:, None] == jnp.arange(w_classes.shape[1], dtype=jnp.int32)[None, :]).astype(
        jnp.float32
    )
    grad_logits = ((probability - onehot) / 64.0).astype(jnp.bfloat16)
    class_term = jnp.dot(mixed_hidden.T, grad_logits, preferred_element_type=jnp.float32)
    grad_classes = lax.psum(class_term, ("gx", "gy"))
    grad_mixed = jnp.dot(grad_logits, w_classes.T, preferred_element_type=jnp.float32).astype(
        jnp.bfloat16
    )
    grad_act = aggregate_back(grad_mixed, graph_parts)
    sigmoid_act = jax.nn.sigmoid(pre_act)
    grad_pre = (grad_act * sigmoid_act * (1.0 + pre_act * (1.0 - sigmoid_act))).astype(jnp.bfloat16)
    grad_all = lax.all_gather(grad_pre, "af", axis=1, tiled=True)
    partial_grad = jnp.dot(mixed_own.T, grad_all, preferred_element_type=jnp.float32)
    grad_hidden = lax.psum(partial_grad, ("gx", "gy"))
    return (grad_hidden, grad_classes)


def solution(mesh):
    placed = (
        P(("gx", "gy"), "af"),
        P(("gx", "gy"), None, None, None),
        P(("gx", "gy"), None),
        P(("gx", "gy"), None),
        P(("gx", "gy")),
        P(("gx", "gy"), None),
        P(("gx", "gy"), None),
        P(("gx", "gy")),
        P("af", None),
        P("af", None),
    )
    return jax.shard_map(
        local, mesh=mesh, in_specs=placed, out_specs=(P("af", None), P("af", None)), check_vma=False
    )
```

profile of v0, /device:TPU:0, one launch (start us, length us, event | category | flops | bytes accessed | tf_op | source)
XLA Modules:
  0.0 358.0 jit_solution(1956559421622123813)
XLA Ops:
  7.2 0.8 iota_compare_fusion.1
  8.0 0.7 compare_select_fusion.3
  8.7 4.8 %gather_fusion.4 = bf16[1536,256]{1,0:T(8,128)(2,1)S(1)} fusion(bf16[1024,256]{1,0:T(8,128)(2,1)S(1)} %copy-done, s32[2048]{0:T(1024)S(1)} %pad_clamp_fusion.1), kind=kCustom, calls=%fused_computation.4 | custom fusion | bytes 1579008 | tf_op jit(solution)/shard_map/gather | solution.py:39
  13.8 0.8 fusion.47
  14.6 2.4 collective-permute-start
  17.0 1.3 collective-permute-start.1
  18.3 4.9 %collective-permute-start.2 = (bf16[1,384,256]{2,1,0:T(8,128)(2,1)}, bf16[1,384,256]{2,1,0:T(8,128)(2,1)}, u32[]{:S(2)}, u32[]{:S(2)}) collective-permute-start(bf16[1,384,256]{2,1,0:T(8,128)(2,1)} %get-tuple-element.14), channel_id=1, source_target_pairs={{0,4},{4,8},{8,12},{1,5},{5,9},{9,13},{2,6},{6,10},{10,14},{3,7},{... | collective-permute-start | bytes 589832 | tf_op jit(solution)/shard_map/ppermute | solution.py:12
  23.2 1.3 collective-permute-start.3
  26.4 1.4 gather_fusion.2
  27.8 0.7 gather_fusion.3
  29.1 0.7 copy-done.11
  30.8 0.7 mul.39
  32.2 0.7 copy-done.13
  33.5 1.3 pad_maximum_fusion
  34.8 10.1 %scatter_custom_fusion = f32[1024,256]{1,0:T(8,128)S(1)} fusion(f32[1024,256]{1,0:T(8,128)S(1)} %bitcast.114, s32[1536]{0:T(1024)} %fusion.39, bf16[1536,256]{1,0:T(8,128)(2,1)S(1)} %bitcast.119, f32[1536]{0:T(1024)S(1)} %mul.39), kind=kCustom, calls=%fused_computation.25 | custom fusion | flops 1179648 | bytes 1843200 | tf_op jit(solution)/shard_map/scatter-add | solution.py:43
  44.9 0.9 convert_element_type.50
  46.3 29.3 %all_to_all.19 = bf16[256,4,256]{0,2,1:T(8,128)(2,1)S(1)} all-to-all(bf16[256,4,256]{0,2,1:T(8,128)(2,1)S(1)} %bitcast.123), channel_id=1, replica_groups=mesh['gx'=2,'gy'=4,'af'=4] {'af'}, dimensions={1} | all-to-all | bytes 1048576 | tf_op jit(solution)/shard_map/all_to_all | solution.py:85
  75.9 27.3 %all-gather.3.cloned.1.call-done = bf16[1024,1024]{1,0:T(8,128)(2,1)} async-done(((bf16[1024,256]{1,0:T(8,128)(2,1)}), bf16[1024,1024]{1,0:T(8,128)(2,1)}) %all-gather.3.cloned.1.call-update) | async-done | bytes 2097168 | tf_op jit(solution)/shard_map/all_gather | solution.py:84
  103.3 3.3 multiply_convert_fusion.1
  106.5 4.8 %gather_fusion.9 = bf16[1536,256]{1,0:T(8,128)(2,1)S(1)} fusion(bf16[1024,256]{1,0:T(8,128)(2,1)S(1)} %get-tuple-element.20, s32[2048]{0:T(1024)S(1)} %pad_clamp_fusion.1), kind=kCustom, calls=%fused_computation.9 | custom fusion | bytes 1579008 | tf_op jit(solution)/shard_map/gather | solution.py:39
  111.3 0.7 gather_fusion.5
  112.0 1.5 gather_fusion.6
  113.5 1.5 gather_fusion.7
  115.0 1.5 gather_fusion.8
  116.9 2.0 collective-permute-start.4
  118.9 1.3 collective-permute-start.5
  120.2 4.2 %collective-permute-start.6 = (bf16[1,384,256]{2,1,0:T(8,128)(2,1)S(1)}, bf16[1,384,256]{2,1,0:T(8,128)(2,1)S(1)}, u32[]{:S(2)}, u32[]{:S(2)}) collective-permute-start(bf16[1,384,256]{2,1,0:T(8,128)(2,1)S(1)} %get-tuple-element.10), channel_id=1, source_target_pairs={{0,4},{4,8},{8,12},{1,5},{5,9},{9,13},{2,6},{6,10},{10,14},{3,7},{... | collective-permute-start | bytes 589832 | tf_op jit(solution)/shard_map/ppermute | solution.py:12
  124.5 1.3 collective-permute-start.7
  126.4 0.7 copy-done.9
  127.4 0.8 copy-done.8
  128.5 1.1 collective-permute-done.6
  129.6 6.4 %collective-permute-done.7 = bf16[1,384,256]{2,1,0:T(8,128)(2,1)S(1)} collective-permute-done((bf16[1,384,256]{2,1,0:T(8,128)(2,1)S(1)}, bf16[1,384,256]{2,1,0:T(8,128)(2,1)S(1)}, u32[]{:S(2)}, u32[]{:S(2)}) %collective-permute-start.7) | collective-permute-done | bytes 196640 | tf_op jit(solution)/shard_map/ppermute | solution.py:15
  136.1 10.3 %scatter_custom_fusion.1 = f32[1024,256]{1,0:T(8,128)S(1)} fusion(f32[1024,256]{1,0:T(8,128)S(1)} %bitcast.115, s32[1536]{0:T(1024)} %fusion.39, bf16[1536,256]{1,0:T(8,128)(2,1)S(1)} %bitcast.118, f32[1536]{0:T(1024)S(1)} %mul.39), kind=kCustom, calls=%fused_computation.23 | custom fusion | flops 1179648 | bytes 1843200 | tf_op jit(solution)/shard_map/scatter-add | solution.py:43
  146.4 1.2 fusion.25
  147.8 37.2 %all-reduce.4.cloned.1.call-done = f32[1024,128]{1,0:T(8,128)} async-done(((f32[1024,128]{1,0:T(8,128)}), f32[1024,128]{1,0:T(8,128)}) %all-reduce.4.cloned.1.call-update) | async-done | bytes 524304 | tf_op jit(solution)/shard_map/psum | solution.py:89
  184.9 1.2 reduce_max.9
  186.2 1.4 fusion.8
  187.6 1.6 convolution_convert_fusion
  189.3 1.3 convolution_bitcast_fusion.3
  190.6 1.3 convolution_bitcast_fusion.2
  192.3 5.3 %gather_fusion.10 = bf16[1536,256]{1,0:T(8,128)(2,1)} fusion(bf16[1024,256]{1,0:T(8,128)(2,1)S(1)} %convolution_convert_fusion, s32[2048]{0:T(1024)S(1)} %pad_clamp_fusion), kind=kCustom, calls=%fused_computation.10 | custom fusion | bytes 1579008 | tf_op jit(solution)/shard_map/gather | solution.py:58
  197.6 1.4 fusion.1
  199.0 0.9 fusion.45
  199.9 1.3 collective-permute-start.10
  201.2 5.2 %collective-permute-start.11 = (bf16[1,384,256]{2,1,0:T(8,128)(2,1)}, bf16[1,384,256]{2,1,0:T(8,128)(2,1)}, u32[]{:S(2)}, u32[]{:S(2)}) collective-permute-start(bf16[1,384,256]{2,1,0:T(8,128)(2,1)} %get-tuple-element.5), channel_id=1, source_target_pairs={{0,4},{4,8},{8,12},{1,5},{5,9},{9,13},{2,6},{6,10},{10,14},{3,7},{... | collective-permute-start | bytes 589832 | tf_op jit(solution)/shard_map/ppermute | solution.py:12
  206.4 1.3 collective-permute-start.8
  207.7 4.4 %collective-permute-start.9 = (bf16[1,384,256]{2,1,0:T(8,128)(2,1)S(1)}, bf16[1,384,256]{2,1,0:T(8,128)(2,1)}, u32[]{:S(2)}, u32[]{:S(2)}) collective-permute-start(bf16[1,384,256]{2,1,0:T(8,128)(2,1)S(1)} %get-tuple-element.7), channel_id=1, source_target_pairs={{0,16},{1,17},{2,18},{3,19},{4,20},{5,21},{6,22},{7,23},{8,24},{9,... | collective-permute-start | bytes 589832 | tf_op jit(solution)/shard_map/ppermute | solution.py:12
  212.1 2.5 copy.43
  214.6 2.5 copy.45
  217.1 1.4 copy.47
  218.8 1.3 copy.49
  220.2 1.1 copy-done.4
  221.4 1.6 scatter_fusion
  223.0 2.5 scatter_fusion.1
  225.5 1.3 scatter_fusion.2
  226.8 2.5 scatter_fusion.3
  229.3 1.2 pad_maximum_fusion.2
  230.6 10.3 %scatter_custom_fusion.6 = f32[1024,256]{1,0:T(8,128)S(1)} fusion(f32[1024,256]{1,0:T(8,128)S(1)} %bitcast.113, s32[1536]{0:T(1024)S(1)} %fusion.40, bf16[1536,256]{1,0:T(8,128)(2,1)S(1)} %bitcast.117, f32[]{:T(128)} %constant.12.clone.1, pred[1536]{0:T(1024)(128)(4,1)S(1)} %lt.83), kind=kCustom, calls=%fused_computation.19 | custom fusion | flops 1179648 | bytes 1837060 | tf_op jit(solution)/shard_map/scatter-add | solution.py:66
  240.9 2.5 multiply_convert_fusion
  243.5 1.4 fusion.23
  245.0 44.2 %all-gather.5.cloned.1.call-done = bf16[1024,1024]{1,0:T(8,128)(2,1)} async-done(((bf16[1024,256]{1,0:T(8,128)(2,1)}), bf16[1024,1024]{1,0:T(8,128)(2,1)}) %all-gather.5.cloned.1.call-update) | async-done | bytes 2097168 | tf_op jit(solution)/shard_map/all_gather | solution.py:104
  289.2 3.3 fusion.48
  292.5 55.9 %all-reduce.6.cloned.1.call-done = (f32[256,1024]{1,0:T(8,128)}, f32[256,128]{1,0:T(8,128)}) async-done(((f32[256,1024]{1,0:T(8,128)}, f32[256,128]{1,0:T(8,128)}), (f32[256,1024]{1,0:T(8,128)}, f32[256,128]{1,0:T(8,128)})) %all-reduce.6.cloned.1.call-update) | async-done | bytes 1179664 | tf_op jit(solution)/shard_map/psum | solution.py:106
  348.4 2.3 copy.70
  (120 shorter events, 9.0 us)
Async XLA Ops:
  7.2 1.6 copy-start
  7.2 96.1 %all-gather.3.cloned.1.call-start = ((), (), s32[]{:S(2)}) async-start(), calls=%async_computation.1 | async-start | bytes 2621440 | tf_op jit(solution)/shard_map/all_gather | solution.py:84
  8.0 5.5 %copy-start.17 = (pred[4,384]{1,0:T(4,128)(4,1)}, pred[4,384]{1,0:T(4,128)(4,1)S(1)}, u32[]{:S(2)}) copy-start(pred[4,384]{1,0:T(4,128)(4,1)S(1)} %iota_compare_fusion.1) | copy-start | bytes 4612
  13.5 11.0 %copy-start.34 = (s32[8,4]{0,1:T(4,128)S(1)}, s32[8,4]{0,1:T(4,128)}, u32[]{:S(2)}) copy-start(s32[8,4]{0,1:T(4,128)} %param.12) | copy-start | bytes 388
  14.6 17.5 %collective-permute-start = (bf16[1,384,256]{2,1,0:T(8,128)(2,1)}, bf16[1,384,256]{2,1,0:T(8,128)(2,1)S(1)}, u32[]{:S(2)}, u32[]{:S(2)}) collective-permute-start(bf16[1,384,256]{2,1,0:T(8,128)(2,1)} %get-tuple-element.12), channel_id=1, source_target_pairs={{0,16},{1,17},{2,18},{3,19},{4,20},{5,21},{6,22},{7,23},{8,24},{9,... | collective-permute-start | bytes 589832 | tf_op jit(solution)/shard_map/ppermute | solution.py:12
  17.0 15.2 %collective-permute-start.1 = (bf16[1,384,256]{2,1,0:T(8,128)(2,1)}, bf16[1,384,256]{2,1,0:T(8,128)(2,1)}, u32[]{:S(2)}, u32[]{:S(2)}) collective-permute-start(bf16[1,384,256]{2,1,0:T(8,128)(2,1)} %get-tuple-element.15), channel_id=1, source_target_pairs={{16,0},{17,1},{18,2},{19,3},{20,4},{21,5},{22,6},{23,7},{24,8},{25... | collective-permute-start | bytes 589832 | tf_op jit(solution)/shard_map/ppermute | solution.py:15
  18.3 13.9 %collective-permute-start.2 = (bf16[1,384,256]{2,1,0:T(8,128)(2,1)}, bf16[1,384,256]{2,1,0:T(8,128)(2,1)}, u32[]{:S(2)}, u32[]{:S(2)}) collective-permute-start(bf16[1,384,256]{2,1,0:T(8,128)(2,1)} %get-tuple-element.14), channel_id=1, source_target_pairs={{0,4},{4,8},{8,12},{1,5},{5,9},{9,13},{2,6},{6,10},{10,14},{3,7},{... | collective-permute-start | bytes 589832 | tf_op jit(solution)/shard_map/ppermute | solution.py:12
  23.2 10.3 %collective-permute-start.3 = (bf16[1,384,256]{2,1,0:T(8,128)(2,1)S(1)}, bf16[1,384,256]{2,1,0:T(8,128)(2,1)}, u32[]{:S(2)}, u32[]{:S(2)}) collective-permute-start(bf16[1,384,256]{2,1,0:T(8,128)(2,1)S(1)} %get-tuple-element.13), channel_id=1, source_target_pairs={{4,0},{8,4},{12,8},{5,1},{9,5},{13,9},{6,2},{10,6},{14,10},{7,3},{... | collective-permute-start | bytes 589832 | tf_op jit(solution)/shard_map/ppermute | solution.py:15
  24.5 3.2 copy-start.25
  24.5 3.2 copy-start.27
  24.5 3.2 copy-start.29
  24.5 3.2 copy-start.31
  24.6 3.2 copy-start.22
  24.6 3.2 copy-start.23
  25.2 3.3 copy-start.1
  26.4 1.4 copy-start.24
  28.8 1.0 copy-start.11
  30.1 0.7 copy-start.19
  32.2 0.7 copy-start.13
  44.9 1.2 copy-start.12
  45.8 139.1 %all-reduce.4.cloned.1.call-start = ((), (), s32[]{:S(2)}) async-start(), calls=%async_computation.2 | async-start | bytes 1048576 | tf_op jit(solution)/shard_map/psum | solution.py:89
  112.0 4.6 %copy-start.18 = (pred[4,384]{1,0:T(4,128)(4,1)S(1)}, pred[4,384]{1,0:T(4,128)(4,1)}, u32[]{:S(2)}) copy-start(pred[4,384]{1,0:T(4,128)(4,1)} %copy-done.17) | copy-start | bytes 4612
  116.8 9.3 %copy-start.10 = (bf16[8,128,256]{2,1,0:T(8,128)(2,1)S(1)}, bf16[8,128,256]{2,1,0:T(8,128)(2,1)}, u32[]{:S(2)}) copy-start(bf16[8,128,256]{2,1,0:T(8,128)(2,1)} %gather_fusion.6) | copy-start | bytes 1572868
  116.9 11.6 %collective-permute-start.4 = (bf16[1,384,256]{2,1,0:T(8,128)(2,1)S(1)}, bf16[1,384,256]{2,1,0:T(8,128)(2,1)S(1)}, u32[]{:S(2)}, u32[]{:S(2)}) collective-permute-start(bf16[1,384,256]{2,1,0:T(8,128)(2,1)S(1)} %get-tuple-element.8), channel_id=1, source_target_pairs={{0,16},{1,17},{2,18},{3,19},{4,20},{5,21},{6,22},{7,23},{8,24},{9,... | collective-permute-start | bytes 589832 | tf_op jit(solution)/shard_map/ppermute | solution.py:12
  118.9 9.5 %collective-permute-start.5 = (bf16[1,384,256]{2,1,0:T(8,128)(2,1)S(1)}, bf16[1,384,256]{2,1,0:T(8,128)(2,1)S(1)}, u32[]{:S(2)}, u32[]{:S(2)}) collective-permute-start(bf16[1,384,256]{2,1,0:T(8,128)(2,1)S(1)} %get-tuple-element.11), channel_id=1, source_target_pairs={{16,0},{17,1},{18,2},{19,3},{20,4},{21,5},{22,6},{23,7},{24,8},{25... | collective-permute-start | bytes 589832 | tf_op jit(solution)/shard_map/ppermute | solution.py:15
  120.2 9.3 %collective-permute-start.6 = (bf16[1,384,256]{2,1,0:T(8,128)(2,1)S(1)}, bf16[1,384,256]{2,1,0:T(8,128)(2,1)S(1)}, u32[]{:S(2)}, u32[]{:S(2)}) collective-permute-start(bf16[1,384,256]{2,1,0:T(8,128)(2,1)S(1)} %get-tuple-element.10), channel_id=1, source_target_pairs={{0,4},{4,8},{8,12},{1,5},{5,9},{9,13},{2,6},{6,10},{10,14},{3,7},{... | collective-permute-start | bytes 589832 | tf_op jit(solution)/shard_map/ppermute | solution.py:12
  124.5 11.5 %collective-permute-start.7 = (bf16[1,384,256]{2,1,0:T(8,128)(2,1)S(1)}, bf16[1,384,256]{2,1,0:T(8,128)(2,1)S(1)}, u32[]{:S(2)}, u32[]{:S(2)}) collective-permute-start(bf16[1,384,256]{2,1,0:T(8,128)(2,1)S(1)} %get-tuple-element.9), channel_id=1, source_target_pairs={{4,0},{8,4},{12,8},{5,1},{9,5},{13,9},{6,2},{10,6},{14,10},{7,3},{... | collective-permute-start | bytes 589832 | tf_op jit(solution)/shard_map/ppermute | solution.py:15
  126.1 1.0 copy-start.9
  127.1 1.0 copy-start.8
  128.5 17.9 %copy-start.15 = (bf16[256,128]{1,0:T(8,128)(2,1)S(1)}, bf16[256,128]{1,0:T(8,128)(2,1)}, u32[]{:S(2)}) copy-start(bf16[256,128]{1,0:T(8,128)(2,1)} %param.19) | copy-start | bytes 196612
  136.1 11.6 %copy-start.20 = (s32[4,384]{1,0:T(4,128)S(1)}, s32[4,384]{1,0:T(4,128)}, u32[]{:S(2)}) copy-start(s32[4,384]{1,0:T(4,128)} %param.15) | copy-start | bytes 18436
  136.1 11.6 %copy-start.21 = (s32[4,384]{1,0:T(4,128)S(1)}, s32[4,384]{1,0:T(4,128)}, u32[]{:S(2)}) copy-start(s32[4,384]{1,0:T(4,128)} %param.13) | copy-start | bytes 18436
  146.4 39.8 %copy-start.5 = (f32[1024,256]{1,0:T(8,128)}, f32[1024,256]{1,0:T(8,128)S(1)}, u32[]{:S(2)}) copy-start(f32[1024,256]{1,0:T(8,128)S(1)} %scatter_custom_fusion.1) | copy-start | bytes 3145732
  146.4 41.2 %copy-start.35 = (s32[1024]{0:T(1024)S(1)}, s32[1024]{0:T(1024)}, u32[]{:S(2)}) copy-start(s32[1024]{0:T(1024)} %param.17) | copy-start | bytes 12292
  147.6 141.6 %all-gather.5.cloned.1.call-start = ((), (), s32[]{:S(2)}) async-start(), calls=%async_computation.3 | async-start | bytes 2621440 | tf_op jit(solution)/shard_map/all_gather | solution.py:104
  187.6 3.0 copy-start.32
  192.3 5.4 %copy-start.16 = (f32[4,384]{1,0:T(4,128)S(1)}, f32[4,384]{1,0:T(4,128)}, u32[]{:S(2)}) copy-start(f32[4,384]{1,0:T(4,128)} %param.16) | copy-start | bytes 18436
  199.9 29.4 %collective-permute-start.10 = (bf16[1,384,256]{2,1,0:T(8,128)(2,1)}, bf16[1,384,256]{2,1,0:T(8,128)(2,1)S(1)}, u32[]{:S(2)}, u32[]{:S(2)}) collective-permute-start(bf16[1,384,256]{2,1,0:T(8,128)(2,1)} %get-tuple-element.6), channel_id=1, source_target_pairs={{4,0},{8,4},{12,8},{5,1},{9,5},{13,9},{6,2},{10,6},{14,10},{7,3},{... | collective-permute-start | bytes 589832 | tf_op jit(solution)/shard_map/ppermute | solution.py:15
  201.2 28.1 %collective-permute-start.11 = (bf16[1,384,256]{2,1,0:T(8,128)(2,1)}, bf16[1,384,256]{2,1,0:T(8,128)(2,1)}, u32[]{:S(2)}, u32[]{:S(2)}) collective-permute-start(bf16[1,384,256]{2,1,0:T(8,128)(2,1)} %get-tuple-element.5), channel_id=1, source_target_pairs={{0,4},{4,8},{8,12},{1,5},{5,9},{9,13},{2,6},{6,10},{10,14},{3,7},{... | collective-permute-start | bytes 589832 | tf_op jit(solution)/shard_map/ppermute | solution.py:12
  206.4 22.9 %collective-permute-start.8 = (bf16[1,384,256]{2,1,0:T(8,128)(2,1)}, bf16[1,384,256]{2,1,0:T(8,128)(2,1)}, u32[]{:S(2)}, u32[]{:S(2)}) collective-permute-start(bf16[1,384,256]{2,1,0:T(8,128)(2,1)} %get-tuple-element.4), channel_id=1, source_target_pairs={{16,0},{17,1},{18,2},{19,3},{20,4},{21,5},{22,6},{23,7},{24,8},{25... | collective-permute-start | bytes 589832 | tf_op jit(solution)/shard_map/ppermute | solution.py:15
  207.7 21.6 %collective-permute-start.9 = (bf16[1,384,256]{2,1,0:T(8,128)(2,1)S(1)}, bf16[1,384,256]{2,1,0:T(8,128)(2,1)}, u32[]{:S(2)}, u32[]{:S(2)}) collective-permute-start(bf16[1,384,256]{2,1,0:T(8,128)(2,1)S(1)} %get-tuple-element.7), channel_id=1, source_target_pairs={{0,16},{1,17},{2,18},{3,19},{4,20},{5,21},{6,22},{7,23},{8,24},{9,... | collective-permute-start | bytes 589832 | tf_op jit(solution)/shard_map/ppermute | solution.py:12
  220.1 1.2 copy-start.4
  221.4 1.6 copy-start.30
  223.0 2.5 copy-start.3
  223.0 2.5 copy-start.28
  225.5 1.3 copy-start.26
  240.9 2.6 copy-start.6
  240.9 2.6 copy-start.7
  240.9 2.6 copy-start.33
  240.9 2.6 copy-start.36
  243.4 45.8 %copy-start.2 = (bf16[1024,256]{1,0:T(8,128)(2,1)S(1)}, bf16[1024,256]{1,0:T(8,128)(2,1)}, u32[]{:S(2)}) copy-start(bf16[1024,256]{1,0:T(8,128)(2,1)} %convert_element_type.50) | copy-start | bytes 1572868
  243.4 105.0 %all-reduce.6.cloned.1.call-start = ((), (), s32[]{:S(2)}) async-start(), calls=%async_computation.4 | async-start | bytes 2359296 | tf_op jit(solution)/shard_map/psum | solution.py:106
  348.4 2.3 copy-start.14
Sparse Core Ops, SparseCore 0:
  45.9 57.2 all-gather.2
  147.7 37.1 all-reduce.3
  243.6 45.5 all-gather.4
  292.9 55.5 all-reduce.5
where the time goes:
time: 359 us; the launch traced here: 358 us
  waiting for transfers between devices  173 us (48%)
  other arithmetic  51.8 us (14%)
  local copies, waits for them, and re-layouts  41.9 us (12%)
  starting transfers between devices  31 us (9%)
  blocking collectives  29.3 us (8%)
  matrix products  16.4 us (5%)
  between operations  14.6 us (4%)
    psum x1, waiting for transfers between devices, local(): grad_hidden = lax.psum(partial_grad, ('gx', 'gy'))  55.9 us
    all_gather x1, waiting for transfers between devices, local(): grad_all = lax.all_gather(grad_pre, 'af', axis=1, tiled=True)  44.2 us
    psum x1, waiting for transfers between devices, local(): lax.psum(jnp.dot(mixed_hidden, w_classes, preferred_element_type=jnp.floa...  37.2 us
    all_to_all x1, blocking collectives, local(): lax.all_to_all(w_hidden, 'af', split_axis=1, concat_axis=0, tiled=True)  29.3 us
    all_gather x1, waiting for transfers between devices, local(): mixed_all = lax.all_gather(mixed_own, 'af', axis=1, tiled=True)  27.3 us
    ppermute x6, starting transfers between devices, with_halo(): lax.ppermute(lax.slice_in_dim(block, block.shape[dim] - width, None, axis...  23.1 us
    scatter-add x2, other arithmetic, aggregate(): local_sum.at[recv_target.reshape(-1)].add(weighted.reshape(-1, feat_width))  20.3 us
    scatter-add x1, other arithmetic, aggregate_back(): local_sum.at[send_rows.reshape(-1)].add(returned.reshape(-1, feat_width))  10.3 us
  transfers between devices with their start and end apart: 16, of which 7 were waited for; matrix products, arithmetic and copies ran while one was open for 7% of the time, Pallas kernels for 0%

commit v1 on v0

v1 whole, which is shorter than its diff:
```python
import functools

import jax
import jax.numpy as jnp
from jax import lax
from jax.experimental import pallas as pl
from jax.experimental.pallas import tpu as pltpu
from jax.sharding import PartitionSpec as P

MESH = pl.DeviceIdType.MESH
BF = jnp.bfloat16
F32 = jnp.float32
CHUNKS = 4


def mm(a, b):
    return jnp.dot(a, b, preferred_element_type=F32)


def mm_tn(a, b):
    return lax.dot_general(a, b, (((0,), (0,)), ((), ())), preferred_element_type=F32)


def mm_nt(a, b):
    return lax.dot_general(a, b, (((1,), (1,)), ((), ())), preferred_element_type=F32)


def kernel(
    sizes,
    feat,
    adj,
    colb,
    row_i,
    col_i,
    col_w,
    labels,
    wh,
    wc,
    out_w,
    out_c,
    send_hot,
    send_hot_t,
    recv_hot,
    recv_hot_t,
    dense,
    dense_t,
    acc,
    field,
    halo_out,
    halo_in,
    gathered,
    w_cols,
    pre,
    mixed_hidden,
    logit_out,
    logit_in,
    grad_logits,
    grad_out,
    grad_in,
    class_out,
    class_in,
    piece_out,
    piece_in,
    whole_w,
    whole_c,
    halo_ss,
    halo_rs,
    up_ss,
    down_ss,
    ag_rs,
    w_ss,
    w_rs,
    lo_ss,
    lo_rs,
    gl_ss,
    gl_rs,
    rs_ss,
    rs_rs,
    cr_ss,
    cr_rs,
    za_ss,
    za_rs,
    fw_ss,
    fw_rs,
    fc_ss,
    fc_rs,
):
    gx, gy, af = sizes
    nodes, width = feat.shape
    slots = col_i.shape[0] // 4
    parts = gx * gy
    rows = width // parts
    quarter = nodes // af
    step = nodes // CHUNKS
    classes = wc.shape[1]
    blocks, tiles, tb, _ = adj.shape
    ix, iy, z = lax.axis_index("gx"), lax.axis_index("gy"), lax.axis_index("af")
    me = ix * gy + iy

    def plane_peer(k):
        px = lax.rem(ix + k // gy, gx)
        py = lax.rem(iy + k % gy, gy)
        return px, py

    def af_peer(k):
        return lax.rem(z + k, af)

    def remote(src, dst, ss, rs, where):
        return pltpu.make_async_remote_copy(
            src_ref=src, dst_ref=dst, send_sem=ss, recv_sem=rs, device_id=where, device_id_type=MESH
        )

    barrier = pltpu.get_barrier_semaphore()
    for k in range(1, parts):
        px, py = plane_peer(k)
        pl.semaphore_signal(barrier, inc=1, device_id=(px, py, z), device_id_type=MESH)
    for k in range(1, af):
        pl.semaphore_signal(barrier, inc=1, device_id=(ix, iy, af_peer(k)), device_id_type=MESH)

    def build_rows(hot, column):
        @pl.loop(0, 4 * slots // 32)
        def _(i):
            at = pl.ds(pl.multiple_of(i * 32, 32), 32)
            ids = col_i[at, column : column + 1]
            lane = lax.broadcasted_iota(jnp.int32, (32, nodes), 1)
            hot[at, :] = jnp.where(lane == ids, 1.0, 0.0).astype(BF)

    def build_cols(hot, row):
        @pl.loop(0, nodes // 32)
        def _(i):
            at = pl.ds(pl.multiple_of(i * 32, 32), 32)
            node = lax.broadcasted_iota(jnp.int32, (32, 4 * slots), 0) + i * 32
            hot[at, :] = jnp.where(node == row_i[row : row + 1, :], 1.0, 0.0).astype(BF)

    build_rows(send_hot, 0)
    pl.semaphore_wait(barrier, parts - 1 + af - 1)

    for k in range(1, af):
        there = af_peer(k)
        remote(
            wh.at[:, pl.ds(pl.multiple_of(there * width, width), width)],
            w_cols.at[z],
            w_ss.at[k],
            w_rs.at[k],
            (ix, iy, there),
        ).start()
    w_cols[z] = wh[:, pl.ds(pl.multiple_of(z * width, width), width)]

    ahead = ((ix + 1 < gx), (ix > 0), (iy + 1 < gy), (iy > 0))
    behind = ((ix > 0), (ix + 1 < gx), (iy > 0), (iy + 1 < gy))
    ahead_id = ((ix + 1, iy, z), (ix - 1, iy, z), (ix, iy + 1, z), (ix, iy - 1, z))
    behind_id = ((ix - 1, iy, z), (ix + 1, iy, z), (ix, iy - 1, z), (ix, iy + 1, z))

    def halo_copy(turn, d, ids):
        return remote(
            halo_out.at[turn, d], halo_in.at[turn, d], halo_ss.at[turn, d], halo_rs.at[turn, d], ids[d]
        )

    def halo_send(turn, source, hot, weighted, targets, ids):
        for d in range(4):
            picked = mm(hot[d * slots : (d + 1) * slots, :], source[...])
            if weighted:
                picked = picked * col_w[d * slots : (d + 1) * slots, :]
            halo_out[turn, d] = picked.astype(BF)

            @pl.when(targets[d])
            def _():
                halo_copy(turn, d, ids).start()

    def halo_take(turn, hot_t, weighted, targets, sources, ids):
        for d in range(4):

            @pl.when(sources[d])
            def _():
                halo_copy(turn, d, ids).wait_recv()

            @pl.when(jnp.logical_not(sources[d]))
            def _():
                halo_in[turn, d] = jnp.zeros((slots, width), BF)

            @pl.when(targets[d])
            def _():
                halo_copy(turn, d, ids).wait_send()

            if weighted:
                scaled = halo_in[turn, d].astype(F32) * col_w[d * slots : (d + 1) * slots, :]
                halo_in[turn, d] = scaled.astype(BF)

        @pl.loop(0, nodes // 256)
        def _(i):
            at = pl.ds(pl.multiple_of(i * 256, 256), 256)
            acc[at, :] += mm(hot_t[at, :], halo_in[turn].reshape(4 * slots, width))

    def local_part(matrix, source):
        @pl.loop(0, nodes // 256)
        def _(i):
            at = pl.ds(pl.multiple_of(i * 256, 256), 256)
            acc[at, :] = mm(matrix[at, :], source[...])

    halo_send(0, feat, send_hot, False, ahead, ahead_id)

    @pl.loop(0, blocks)
    def _(r):
        values = [adj[r, k].astype(F32) for k in range(tiles)]
        turned = [v.T for v in values]
        across = pl.ds(pl.multiple_of(r * tb, tb), tb)
        for c in range(blocks):
            gates = [jnp.where(colb[r, k] == c, 1.0, 0.0).astype(F32) for k in range(tiles)]
            dense[across, c * tb : (c + 1) * tb] = sum(v * g for v, g in zip(values, gates)).astype(BF)
            dense_t[c * tb : (c + 1) * tb, across] = sum(v * g for v, g in zip(turned, gates)).astype(BF)

    local_part(dense, feat)
    build_cols(recv_hot_t, 1)
    halo_take(0, recv_hot_t, True, ahead, behind, ahead_id)

    def up(s, c):
        at = pl.ds(c * step, step)
        return remote(
            gathered.at[s, at], gathered.at[s, at], up_ss.at[s, c], ag_rs.at[s, c], (ix, iy, z + 1)
        )

    def down(s, c):
        at = pl.ds(c * step, step)
        return remote(
            gathered.at[s, at], gathered.at[s, at], down_ss.at[s, c], ag_rs.at[s, c], (ix, iy, z - 1)
        )

    for c in range(CHUNKS):
        gathered[z, c * step : (c + 1) * step] = acc[c * step : (c + 1) * step].astype(BF)

        @pl.when(z + 1 < af)
        def _():
            up(z, c).start()

        @pl.when(z > 0)
        def _():
            down(z, c).start()

    for k in range(1, af):
        here = lax.rem(z - k + af, af)
        remote(w_cols.at[here], w_cols.at[here], w_ss.at[k], w_rs.at[k], (ix, iy, here)).wait_recv()
    for c in range(CHUNKS):
        at = slice(c * step, (c + 1) * step)
        pre[at, :] = mm(gathered[z, at], w_cols[z])
    build_cols(send_hot_t, 0)
    build_rows(recv_hot, 1)
    for k in range(1, af):
        for c in range(CHUNKS):
            at = slice(c * step, (c + 1) * step)

            @pl.when(z - k >= 0)
            def _():
                up(z - k, c).wait_recv()

                @pl.when(z + 1 < af)
                def _():
                    up(z - k, c).start()

                pre[at, :] += mm(gathered[z - k, at], w_cols[z - k])

            @pl.when(z + k < af)
            def _():
                down(z + k, c).wait_recv()

                @pl.when(z > 0)
                def _():
                    down(z + k, c).start()

                pre[at, :] += mm(gathered[z + k, at], w_cols[z + k])

    @pl.loop(0, nodes // 64)
    def _(i):
        at = pl.ds(pl.multiple_of(i * 64, 64), 64)
        v = pre[at, :]
        field[at, :] = (v * jax.nn.sigmoid(v)).astype(BF)

    halo_send(1, field, send_hot, False, ahead, ahead_id)
    local_part(dense, field)
    halo_take(1, recv_hot_t, True, ahead, behind, ahead_id)
    mixed_hidden[...] = acc[...].astype(BF)
    for j in range(af):
        at = slice(j * quarter, (j + 1) * quarter)
        logit_out[j] = mm(mixed_hidden[at, :], wc[...]).astype(BF)
    for k in range(1, af):
        there = af_peer(k)
        remote(
            logit_out.at[there], logit_in.at[k], lo_ss.at[k], lo_rs.at[k], (ix, iy, there)
        ).start()
    mine = pl.ds(pl.multiple_of(z * quarter, quarter), quarter)
    logits = mm(mixed_hidden[mine, :], wc[...])
    for k in range(1, af):
        remote(logit_out.at[z], logit_in.at[k], lo_ss.at[k], lo_rs.at[k], (ix, iy, af_peer(k))).wait()
        logits = logits + logit_in[k].astype(F32)
    exponent = jnp.exp(logits - jnp.max(logits, axis=1, keepdims=True))
    probability = exponent / jnp.sum(exponent, axis=1, keepdims=True)
    lane = lax.broadcasted_iota(jnp.int32, (quarter, classes), 1)
    onehot = jnp.where(lane == labels[mine, :], 1.0, 0.0)
    grad_logits[z] = ((probability - onehot) * (1.0 / 64.0)).astype(BF)
    for k in range(1, af):
        remote(
            grad_logits.at[z], grad_logits.at[z], gl_ss.at[k], gl_rs.at[k], (ix, iy, af_peer(k))
        ).start()
    for k in range(1, af):
        here = lax.rem(z - k + af, af)
        remote(
            grad_logits.at[here], grad_logits.at[here], gl_ss.at[k], gl_rs.at[k], (ix, iy, here)
        ).wait_recv()
    for j in range(af):
        field[j * quarter : (j + 1) * quarter, :] = mm_nt(grad_logits[j], wc[...]).astype(BF)

    halo_send(2, field, recv_hot, True, behind, behind_id)
    class_term = mm_tn(mixed_hidden[...], grad_logits[...].reshape(nodes, classes))
    class_out[...] = class_term.astype(BF).reshape(parts, rows, classes)
    for k in range(1, parts):
        px, py = plane_peer(k)
        remote(
            class_out.at[px * gy + py], class_in.at[k], cr_ss.at[k], cr_rs.at[k], (px, py, z)
        ).start()
    local_part(dense_t, field)
    halo_take(2, send_hot_t, False, behind, ahead, behind_id)

    @pl.loop(0, nodes // 64)
    def _(i):
        at = pl.ds(pl.multiple_of(i * 64, 64), 64)
        v = pre[at, :]
        sig = jax.nn.sigmoid(v)
        field[at, :] = (acc[at, :] * sig * (1.0 + v * (1.0 - sig))).astype(BF)

    for s in range(af):
        term = mm_tn(gathered[s], field[...])
        grad_out[:, s] = term.astype(BF).reshape(parts, rows, width)
    for k in range(1, parts):
        px, py = plane_peer(k)
        remote(
            grad_out.at[px * gy + py], grad_in.at[k], rs_ss.at[k], rs_rs.at[k], (px, py, z)
        ).start()
    class_sum = class_out[me].astype(F32)
    for k in range(1, parts):
        px, py = plane_peer(k)
        remote(class_out.at[me], class_in.at[k], cr_ss.at[k], cr_rs.at[k], (px, py, z)).wait()
        class_sum = class_sum + class_in[k].astype(F32)
    whole_c[me] = class_sum.astype(BF)
    for k in range(1, parts):
        px, py = plane_peer(k)
        remote(whole_c.at[me], whole_c.at[me], fc_ss.at[k], fc_rs.at[k], (px, py, z)).start()
    for k in range(1, parts):
        px, py = plane_peer(k)
        remote(grad_out.at[me], grad_in.at[k], rs_ss.at[k], rs_rs.at[k], (px, py, z)).wait()
    for s in range(af):
        total = grad_out[me, s].astype(F32)
        for k in range(1, parts):
            total = total + grad_in[k, s].astype(F32)
        piece_out[s] = total.astype(BF)
    for k in range(1, af):
        there = af_peer(k)
        remote(
            piece_out.at[there], piece_in.at[z], za_ss.at[k], za_rs.at[k], (ix, iy, there)
        ).start()
    piece_in[z] = piece_out[z]
    for k in range(1, af):
        here = lax.rem(z - k + af, af)
        remote(piece_in.at[here], piece_in.at[here], za_ss.at[k], za_rs.at[k], (ix, iy, here)).wait_recv()
    for s in range(af):
        whole_w[me, s] = piece_in[s]
    for k in range(1, parts):
        px, py = plane_peer(k)
        remote(whole_w.at[me], whole_w.at[me], fw_ss.at[k], fw_rs.at[k], (px, py, z)).start()

    for k in range(1, af):
        remote(w_cols.at[z], w_cols.at[z], w_ss.at[k], w_rs.at[k], (ix, iy, af_peer(k))).wait_send()
        remote(
            grad_logits.at[z], grad_logits.at[z], gl_ss.at[k], gl_rs.at[k], (ix, iy, af_peer(k))
        ).wait_send()
        remote(piece_out.at[z], piece_in.at[z], za_ss.at[k], za_rs.at[k], (ix, iy, af_peer(k))).wait_send()
    for s in range(af):
        for c in range(CHUNKS):

            @pl.when(jnp.logical_and(s <= z, z + 1 < af))
            def _():
                up(s, c).wait_send()

            @pl.when(jnp.logical_and(s >= z, z > 0))
            def _():
                down(s, c).wait_send()

    for k in range(1, parts):
        px = lax.rem(ix - k // gy + gx, gx)
        py = lax.rem(iy - k % gy + gy, gy)
        slot = px * gy + py
        remote(whole_c.at[slot], whole_c.at[slot], fc_ss.at[k], fc_rs.at[k], (px, py, z)).wait()
        remote(whole_w.at[slot], whole_w.at[slot], fw_ss.at[k], fw_rs.at[k], (px, py, z)).wait()
    out_c[...] = whole_c[...]
    for s in range(af):
        out_w[:, :, s * width : (s + 1) * width] = whole_w[:, s]


def local(
    sizes,
    features,
    adj_tiles,
    col_block,
    send_rows,
    send_counts,
    recv_target,
    edge_weight,
    labels,
    w_hidden,
    w_classes,
):
    gx, gy, af = sizes
    parts = gx * gy
    nodes, width = features.shape
    slots = send_rows.shape[1]
    classes = w_classes.shape[1]
    rows = width // parts
    live = jnp.arange(slots, dtype=jnp.int32)[None, :] < send_counts[:, None]
    both = jnp.stack([jnp.where(live, send_rows, -1).reshape(-1), recv_target.reshape(-1)])
    vmem = pl.BlockSpec(memory_space=pltpu.VMEM)
    smem = pl.BlockSpec(memory_space=pltpu.SMEM)
    dma = pltpu.SemaphoreType.DMA
    grad_w, grad_c = pl.pallas_call(
        functools.partial(kernel, sizes),
        out_shape=(
            jax.ShapeDtypeStruct((parts, rows, af * width), BF),
            jax.ShapeDtypeStruct((parts, rows, classes), BF),
        ),
        in_specs=[vmem, vmem, smem, vmem, vmem, vmem, vmem, vmem, vmem],
        out_specs=(vmem, vmem),
        scratch_shapes=[
            pltpu.VMEM((4 * slots, nodes), BF),
            pltpu.VMEM((nodes, 4 * slots), BF),
            pltpu.VMEM((4 * slots, nodes), BF),
            pltpu.VMEM((nodes, 4 * slots), BF),
            pltpu.VMEM((nodes, nodes), BF),
            pltpu.VMEM((nodes, nodes), BF),
            pltpu.VMEM((nodes, width), F32),
            pltpu.VMEM((nodes, width), BF),
            pltpu.VMEM((3, 4, slots, width), BF),
            pltpu.VMEM((3, 4, slots, width), BF),
            pltpu.VMEM((af, nodes, width), BF),
            pltpu.VMEM((af, width, width), BF),
            pltpu.VMEM((nodes, width), F32),
            pltpu.VMEM((nodes, width), BF),
            pltpu.VMEM((af, nodes // af, classes), BF),
            pltpu.VMEM((af, nodes // af, classes), BF),
            pltpu.VMEM((af, nodes // af, classes), BF),
            pltpu.VMEM((parts, af, rows, width), BF),
            pltpu.VMEM((parts, af, rows, width), BF),
            pltpu.VMEM((parts, rows, classes), BF),
            pltpu.VMEM((parts, rows, classes), BF),
            pltpu.VMEM((af, rows, width), BF),
            pltpu.VMEM((af, rows, width), BF),
            pltpu.VMEM((parts, af, rows, width), BF),
            pltpu.VMEM((parts, rows, classes), BF),
            dma((3, 4)),
            dma((3, 4)),
            dma((af, CHUNKS)),
            dma((af, CHUNKS)),
            dma((af, CHUNKS)),
            dma((af,)),
            dma((af,)),
            dma((af,)),
            dma((af,)),
            dma((af,)),
            dma((af,)),
            dma((parts,)),
            dma((parts,)),
            dma((parts,)),
            dma((parts,)),
            dma((af,)),
            dma((af,)),
            dma((parts,)),
            dma((parts,)),
            dma((parts,)),
            dma((parts,)),
        ],
        compiler_params=pltpu.CompilerParams(
            collective_id=0, has_side_effects=True, vmem_limit_bytes=56 * 1024 * 1024
        ),
        name="gcn_step",
    )(
        features,
        adj_tiles,
        col_block,
        both,
        both.T,
        edge_weight.reshape(-1, 1),
        labels.reshape(-1, 1),
        w_hidden,
        w_classes,
    )
    return (
        grad_w.reshape(width, af * width).astype(F32),
        grad_c.reshape(width, classes).astype(F32),
    )


def solution(mesh):
    sizes = (mesh.shape["gx"], mesh.shape["gy"], mesh.shape["af"])
    placed = (
        P(("gx", "gy"), "af"),
        P(("gx", "gy"), None, None, None),
        P(("gx", "gy"), None),
        P(("gx", "gy"), None),
        P(("gx", "gy")),
        P(("gx", "gy"), None),
        P(("gx", "gy"), None),
        P(("gx", "gy")),
        P("af", None),
        P("af", None),
    )
    return jax.shard_map(
        functools.partial(local, sizes),
        mesh=mesh,
        in_specs=placed,
        out_specs=(P("af", None), P("af", None)),
        check_vma=False,
    )
```

time: 359 us -> 123 us (0.34)
  waiting for transfers between devices: 173 us -> 0 us
  Pallas kernels: 0 us -> 111 us
  other arithmetic: 51.8 us -> 3.72 us
  local copies, waits for them, and re-layouts: 41.9 us -> 6.82 us
  starting transfers between devices: 31 us -> 0 us
  blocking collectives: 29.3 us -> 0 us
  matrix products: 16.4 us -> 0 us
  between operations: 14.6 us -> 0.68 us
    pallas_call x0 -> x1, Pallas kernels: none -> 111 us  [local(): pl.pallas_call(functools.partial(kernel, sizes), out_shape=(jax.ShapeDtyp...]
    psum x2 -> x0, waiting for transfers between devices: 93.1 us -> none  [the longest x1 55.9 us: local(): grad_hidden = lax.psum(partial_grad, ('gx', 'gy'))]
    all_gather x2 -> x0, waiting for transfers between devices: 71.6 us -> none  [the longest x1 44.2 us: local(): grad_all = lax.all_gather(grad_pre, 'af', axis=1, tiled=True)]
    scatter-add x7 -> x0, other arithmetic: 38.5 us -> none  [the longest x2 20.3 us: aggregate(): local_sum.at[recv_target.reshape(-1)].add(weighted.reshape(-1, feat_width))]
    ppermute x12 -> x0, starting transfers between devices: 30.8 us -> none  [the longest x6 23.1 us: with_halo(): lax.ppermute(lax.slice_in_dim(block, block.shape[dim] - width, None, axis...]
    all_to_all x1 -> x0, blocking collectives: 29.3 us -> none  [local(): lax.all_to_all(w_hidden, 'af', split_axis=1, concat_axis=0, tiled=True)]
    gather x11 -> x0, local copies, waits for them, and re-layouts: 23.3 us -> none  [the longest x2 9.51 us: aggregate(): node_field[send_rows]]
    dot_general x17 -> x0, matrix products: 16.4 us -> none  [the longest x4 3.34 us: aggregate_back(): jnp.einsum('bij,bif->bjf', adj_tiles[:, slot], grad_blocks, preferred_ele...]
  transfers between devices with their start and end apart: 16 -> 0, of which waited for: 7 -> 0; matrix products, arithmetic and copies ran while one was open for 7% -> 0% of each run, Pallas kernels for 0% -> 0%
where the time goes in v1:
time: 123 us; the launch traced here: 122 us
  Pallas kernels  111 us (90%)
  local copies, waits for them, and re-layouts  6.82 us (6%)
  other arithmetic  3.72 us (3%)
    pallas_call x1, Pallas kernels, local(): pl.pallas_call(functools.partial(kernel, sizes), out_shape=(jax.ShapeDtyp...  111 us
    unnamed x17, local copies, waits for them, and re-layouts  4.61 us

profile of v1, /device:TPU:0, one launch (start us, length us, event | category | flops | bytes accessed | tf_op | source)
XLA Modules:
  0.0 122.5 jit_solution(12416677523816687687)
XLA Ops:
  0.6 0.0 copy-start.1
  0.6 0.0 copy-start.5
  0.7 1.4 %copy.21.colb = s32[8,4]{1,0:T(8,128)} copy(s32[8,4]{0,1:T(4,128)} %param.12) | data formatting | bytes 256 | tf_op args[2]
  2.0 0.0 copy-done.1
  2.0 0.0 copy-done.5
  2.0 0.1 select_bitcast_fusion
  2.1 0.0 copy-start.2
  2.1 0.7 copy-done.2
  2.8 0.0 copy-start.3
  2.8 0.7 copy-done.3
  3.5 0.0 copy-start
  3.5 0.0 copy-start.4
  3.5 0.7 copy-done.4
  4.2 1.0 copy.23.labels
  5.2 1.2 copy.27
  6.4 0.0 copy-done
  6.4 1.2 copy.20
  7.6 111.2 %gcn_step.1 = (bf16[8,32,1024]{2,1,0:T(8,128)(2,1)}, bf16[8,32,128]{2,1,0:T(8,128)(2,1)}) custom-call(bf16[1024,256]{1,0:T(8,128)(2,1)} %feat.1, bf16[8,4,128,128]{3,2,1,0:T(8,128)(2,1)} %adj.1, s32[8,4]{1,0:T(8,128)} %copy.21.colb, s32[2,1536]{1,0:T(2,128)} %copy-done, s32[1536,2]{1,0:T(8,128)} %bitcast.20, f32[1536,1]{1,0:T(8,128)} %bitcast.19, ...), custom_call_target="tpu_custom_call" | custom-call | tf_op jit(solution)/shard_map/gcn_step/pallas_call | solution.py:421
  118.8 1.5 %bitcast_convert_fusion.1 = f32[256,128]{1,0:T(8,128)} fusion(bf16[8,32,128]{2,1,0:T(8,128)(2,1)} %get-tuple-element.5), kind=kLoop, calls=%fused_computation.1 | loop fusion | flops 32768 | bytes 196608 | tf_op jit(solution)/shard_map/convert_element_type | solution.py:494
  120.3 2.1 %bitcast_convert_fusion = f32[256,1024]{1,0:T(8,128)} fusion(bf16[8,32,1024]{2,1,0:T(8,128)(2,1)} %get-tuple-element.4), kind=kLoop, calls=%fused_computation | loop fusion | flops 262144 | bytes 1572864 | tf_op jit(solution)/shard_map/convert_element_type | solution.py:493
  (4 shorter events, 0.0 us)
Async XLA Ops:
  0.6 1.4 %copy-start.1 = (s32[4,384]{1,0:T(4,128)S(1)}, s32[4,384]{1,0:T(4,128)}, u32[]{:S(2)}) copy-start(s32[4,384]{1,0:T(4,128)} %param.13) | copy-start | bytes 18436
  0.6 1.4 %copy-start.5 = (s32[4]{0:T(128)S(1)}, s32[4]{0:T(128)}, u32[]{:S(2)}) copy-start(s32[4]{0:T(128)} %param.14) | copy-start | bytes 52
  2.1 0.7 copy-start.2
  2.8 0.7 copy-start.3
  3.5 2.9 %copy-start = (s32[2,1536]{1,0:T(2,128)}, s32[2,1536]{1,0:T(2,128)S(1)}, u32[]{:S(2)}) copy-start(s32[2,1536]{1,0:T(2,128)S(1)} %pad_add_fusion.row_i) | copy-start | bytes 36868
  3.5 0.7 copy-start.4

commit v2 on v1

v2 whole, which is shorter than its diff:
```python
import functools

import jax
import jax.numpy as jnp
from jax import lax
from jax.experimental import pallas as pl
from jax.experimental.pallas import tpu as pltpu
from jax.sharding import PartitionSpec as P

MESH = pl.DeviceIdType.MESH
BF = jnp.bfloat16
F32 = jnp.float32
CHUNKS = 4


def mm(a, b):
    return jnp.dot(a, b, preferred_element_type=F32)


def mm_tn(a, b):
    return lax.dot_general(a, b, (((0,), (0,)), ((), ())), preferred_element_type=F32)


def mm_nt(a, b):
    return lax.dot_general(a, b, (((1,), (1,)), ((), ())), preferred_element_type=F32)


def kernel(
    sizes,
    feat,
    adj,
    colb,
    send_rows,
    counts,
    recv_rows,
    weights,
    labels,
    wh,
    wc,
    out_w,
    out_c,
    send_hot,
    send_hot_t,
    recv_hot,
    recv_hot_t,
    columns,
    scales,
    dense,
    dense_t,
    acc,
    field,
    halo_out,
    halo_in,
    halo_low,
    gathered,
    w_cols,
    pre,
    mixed_hidden,
    logit_out,
    logit_in,
    grad_logits,
    grad_out,
    grad_in,
    class_out,
    class_in,
    piece_out,
    whole_w,
    whole_c,
    halo_ss,
    halo_rs,
    up_ss,
    down_ss,
    ag_rs,
    w_ss,
    w_rs,
    lo_ss,
    lo_rs,
    gl_ss,
    gl_rs,
    rs_ss,
    rs_rs,
    cr_ss,
    cr_rs,
    za_ss,
    za_rs,
    fw_ss,
    fw_rs,
    fc_ss,
    fc_rs,
):
    gx, gy, af = sizes
    nodes, width = feat.shape
    slots = send_rows.shape[1]
    parts = gx * gy
    rows = width // parts
    quarter = nodes // af
    step = nodes // CHUNKS
    classes = wc.shape[1]
    blocks, tiles, tb, _ = adj.shape
    ix, iy, z = lax.axis_index("gx"), lax.axis_index("gy"), lax.axis_index("af")
    me = ix * gy + iy

    def plane_peer(k):
        px = lax.rem(ix + k // gy, gx)
        py = lax.rem(iy + k % gy, gy)
        return px, py

    def af_peer(k):
        return lax.rem(z + k, af)

    def remote(src, dst, ss, rs, where):
        return pltpu.make_async_remote_copy(
            src_ref=src, dst_ref=dst, send_sem=ss, recv_sem=rs, device_id=where, device_id_type=MESH
        )

    barrier = pltpu.get_barrier_semaphore()
    for k in range(1, parts):
        px, py = plane_peer(k)
        pl.semaphore_signal(barrier, inc=1, device_id=(px, py, z), device_id_type=MESH)
    for k in range(1, af):
        pl.semaphore_signal(barrier, inc=1, device_id=(ix, iy, af_peer(k)), device_id_type=MESH)

    lane = lax.broadcasted_iota(jnp.int32, (1, slots), 1)
    live = [jnp.where(lane < counts[d], send_rows[d : d + 1, :], -1) for d in range(4)]
    taken = [recv_rows[d : d + 1, :] for d in range(4)]
    columns[...] = jnp.concatenate([v.astype(F32) for v in live + taken], axis=0).T
    scales[...] = jnp.concatenate([weights[...], weights[...]], axis=0).T

    def build_rows(hot, first):
        for d in range(4):

            @pl.loop(0, slots // 32)
            def _(i):
                at = pl.multiple_of(i * 32, 32)
                ids = columns[pl.ds(at, 32), first + d : first + d + 1].astype(jnp.int32)
                node = lax.broadcasted_iota(jnp.int32, (32, nodes), 1)
                hot[pl.ds(at + d * slots, 32), :] = jnp.where(node == ids, 1.0, 0.0).astype(BF)

    def build_cols(hot, rows_of):
        @pl.loop(0, nodes // 32)
        def _(i):
            at = pl.ds(pl.multiple_of(i * 32, 32), 32)
            node = lax.broadcasted_iota(jnp.int32, (32, slots), 0) + i * 32
            for d in range(4):
                hot[at, d * slots : (d + 1) * slots] = jnp.where(node == rows_of[d], 1.0, 0.0).astype(BF)

    build_rows(send_hot, 0)
    pl.semaphore_wait(barrier, parts - 1 + af - 1)

    for k in range(1, af):
        there = af_peer(k)
        remote(
            wh.at[:, pl.ds(pl.multiple_of(there * width, width), width)],
            w_cols.at[z],
            w_ss.at[k],
            w_rs.at[k],
            (ix, iy, there),
        ).start()
    w_cols[z] = wh[:, pl.ds(pl.multiple_of(z * width, width), width)]

    ahead = ((ix + 1 < gx), (ix > 0), (iy + 1 < gy), (iy > 0))
    behind = ((ix > 0), (ix + 1 < gx), (iy > 0), (iy + 1 < gy))
    ahead_id = ((ix + 1, iy, z), (ix - 1, iy, z), (ix, iy + 1, z), (ix, iy - 1, z))
    behind_id = ((ix - 1, iy, z), (ix + 1, iy, z), (ix, iy - 1, z), (ix, iy + 1, z))

    def halo_copy(turn, d, ids):
        return remote(
            halo_out.at[turn, d], halo_in.at[turn, d], halo_ss.at[turn, d], halo_rs.at[turn, d], ids[d]
        )

    def halo_send(turn, source, hot, weighted, targets, ids):
        for d in (2, 3, 0, 1):
            picked = mm(hot[d * slots : (d + 1) * slots, :], source[...])
            if weighted:
                picked = picked * scales[:, d : d + 1]
            halo_out[turn, d] = picked.astype(BF)

            @pl.when(targets[d])
            def _():
                halo_copy(turn, d, ids).start()

    def halo_take(turn, hot_t, weighted, targets, sources, ids, finish):
        for pair in ((0, 1), (2, 3)):
            for d in pair:

                @pl.when(sources[d])
                def _():
                    halo_copy(turn, d, ids).wait_recv()

                @pl.when(jnp.logical_not(sources[d]))
                def _():
                    halo_in[turn, d] = jnp.zeros((slots, width), BF)

                if weighted:
                    scaled = halo_in[turn, d].astype(F32) * scales[:, d : d + 1]
                    high = scaled.astype(BF)
                    halo_in[turn, d] = high
                    halo_low[d] = (scaled - high.astype(F32)).astype(BF)
            first, last = pair[0] * slots, (pair[1] + 1) * slots

            def add(at):
                hot_part = hot_t[at, first:last]
                total = acc[at, :] + mm(hot_part, halo_in[turn, pair[0] : pair[1] + 1].reshape(-1, width))
                if weighted:
                    total += mm(hot_part, halo_low[pair[0] : pair[1] + 1].reshape(-1, width))
                return total

            if pair[0] == 0:

                @pl.loop(0, nodes // 256)
                def _(i):
                    at = pl.ds(pl.multiple_of(i * 256, 256), 256)
                    acc[at, :] = add(at)

            else:
                finish(add)
        for d in range(4):

            @pl.when(targets[d])
            def _():
                halo_copy(turn, d, ids).wait_send()

    def local_part(matrix, source):
        @pl.loop(0, nodes // 256)
        def _(i):
            at = pl.ds(pl.multiple_of(i * 256, 256), 256)
            acc[at, :] = mm(matrix[at, :], source[...])

    halo_send(0, feat, send_hot, False, ahead, ahead_id)

    @pl.loop(0, blocks)
    def _(r):
        values = [adj[r, k].astype(F32) for k in range(tiles)]
        turned = [v.T for v in values]
        chosen = colb[pl.ds(r, 1), :]
        across = pl.ds(pl.multiple_of(r * tb, tb), tb)
        for c in range(blocks):
            gates = [jnp.where(chosen[:, k : k + 1] == c, 1.0, 0.0) for k in range(tiles)]
            dense[across, c * tb : (c + 1) * tb] = sum(v * g for v, g in zip(values, gates)).astype(BF)
            dense_t[c * tb : (c + 1) * tb, across] = sum(v * g for v, g in zip(turned, gates)).astype(BF)

    local_part(dense, feat)
    build_cols(recv_hot_t, taken)

    def up(s, c):
        at = pl.ds(c * step, step)
        return remote(
            gathered.at[s, at], gathered.at[s, at], up_ss.at[s, c], ag_rs.at[s, c], (ix, iy, z + 1)
        )

    def down(s, c):
        at = pl.ds(c * step, step)
        return remote(
            gathered.at[s, at], gathered.at[s, at], down_ss.at[s, c], ag_rs.at[s, c], (ix, iy, z - 1)
        )

    def spread(add):
        for c in range(CHUNKS):
            gathered[z, c * step : (c + 1) * step] = add(slice(c * step, (c + 1) * step)).astype(BF)

            @pl.when(z + 1 < af)
            def _():
                up(z, c).start()

            @pl.when(z > 0)
            def _():
                down(z, c).start()

    halo_take(0, recv_hot_t, True, ahead, behind, ahead_id, spread)
    for k in range(1, af):
        here = lax.rem(z - k + af, af)
        remote(w_cols.at[here], w_cols.at[here], w_ss.at[k], w_rs.at[k], (ix, iy, here)).wait_recv()
    for c in range(CHUNKS):
        at = slice(c * step, (c + 1) * step)
        pre[at, :] = mm(gathered[z, at], w_cols[z])
    build_cols(send_hot_t, live)
    build_rows(recv_hot, 4)
    for k in range(1, af):
        for c in range(CHUNKS):
            at = slice(c * step, (c + 1) * step)

            @pl.when(z - k >= 0)
            def _():
                up(z - k, c).wait_recv()

                @pl.when(z + 1 < af)
                def _():
                    up(z - k, c).start()

                pre[at, :] += mm(gathered[z - k, at], w_cols[z - k])

            @pl.when(z + k < af)
            def _():
                down(z + k, c).wait_recv()

                @pl.when(z > 0)
                def _():
                    down(z + k, c).start()

                pre[at, :] += mm(gathered[z + k, at], w_cols[z + k])

    @pl.loop(0, nodes // 64)
    def _(i):
        at = pl.ds(pl.multiple_of(i * 64, 64), 64)
        v = pre[at, :]
        field[at, :] = (v * jax.nn.sigmoid(v)).astype(BF)

    halo_send(1, field, send_hot, False, ahead, ahead_id)
    local_part(dense, field)
    own_logits = []

    def to_classes(add):
        for k in (*range(1, af), 0):
            there = af_peer(k)
            at = pl.ds(pl.multiple_of(there * quarter, quarter), quarter)
            mixed = add(at).astype(BF)
            mixed_hidden[at, :] = mixed
            part = mm(mixed, wc[...])
            if k == 0:
                own_logits.append(part)
            else:
                logit_out[there] = part.astype(BF)
                remote(
                    logit_out.at[there], logit_in.at[k], lo_ss.at[k], lo_rs.at[k], (ix, iy, there)
                ).start()

    halo_take(1, recv_hot_t, True, ahead, behind, ahead_id, to_classes)
    logits = own_logits[0]
    for k in range(1, af):
        remote(logit_out.at[z], logit_in.at[k], lo_ss.at[k], lo_rs.at[k], (ix, iy, af_peer(k))).wait()
        logits = logits + logit_in[k].astype(F32)
    exponent = jnp.exp(logits - jnp.max(logits, axis=1, keepdims=True))
    probability = exponent / jnp.sum(exponent, axis=1, keepdims=True)
    mine = pl.ds(pl.multiple_of(z * quarter, quarter), quarter)
    kind = lax.broadcasted_iota(jnp.int32, (classes, quarter), 0)
    onehot = jnp.where(kind == labels[:, mine], 1.0, 0.0).T
    grad_logits[z] = ((probability - onehot) * (1.0 / 64.0)).astype(BF)
    for k in range(1, af):
        remote(
            grad_logits.at[z], grad_logits.at[z], gl_ss.at[k], gl_rs.at[k], (ix, iy, af_peer(k))
        ).start()
    field[mine, :] = mm_nt(grad_logits[z], wc[...]).astype(BF)
    for k in range(1, af):
        here = lax.rem(z - k + af, af)
        remote(
            grad_logits.at[here], grad_logits.at[here], gl_ss.at[k], gl_rs.at[k], (ix, iy, here)
        ).wait_recv()
        at = pl.ds(pl.multiple_of(here * quarter, quarter), quarter)
        field[at, :] = mm_nt(grad_logits[here], wc[...]).astype(BF)

    halo_send(2, field, recv_hot, True, behind, behind_id)
    class_term = mm_tn(mixed_hidden[...], grad_logits[...].reshape(nodes, classes))
    class_out[...] = class_term.astype(BF).reshape(parts, rows, classes)
    for k in range(1, parts):
        px, py = plane_peer(k)
        remote(
            class_out.at[px * gy + py], class_in.at[k], cr_ss.at[k], cr_rs.at[k], (px, py, z)
        ).start()
    local_part(dense_t, field)
    def to_grad_pre(add):
        @pl.loop(0, nodes // 128)
        def _(i):
            at = pl.ds(pl.multiple_of(i * 128, 128), 128)
            v = pre[at, :]
            sig = jax.nn.sigmoid(v)
            field[at, :] = (add(at) * sig * (1.0 + v * (1.0 - sig))).astype(BF)

    halo_take(2, send_hot_t, False, behind, ahead, behind_id, to_grad_pre)

    def piece(k, j, slot):
        px, py = plane_peer(j)
        return remote(
            grad_out.at[k, slot], grad_in.at[k, j], rs_ss.at[k, j], rs_rs.at[k, j], (px, py, z)
        )

    order = (*range(1, af), 0)
    for k in order:
        term = mm_tn(gathered[af_peer(k)], field[...])
        grad_out[k] = term.astype(BF).reshape(parts, rows, width)
        for j in range(1, parts):
            px, py = plane_peer(j)
            piece(k, j, px * gy + py).start()
    class_sum = class_out[me].astype(F32)
    for k in range(1, parts):
        px, py = plane_peer(k)
        remote(class_out.at[me], class_in.at[k], cr_ss.at[k], cr_rs.at[k], (px, py, z)).wait()
        class_sum = class_sum + class_in[k].astype(F32)
    whole_c[me] = class_sum.astype(BF)
    for k in range(1, parts):
        px, py = plane_peer(k)
        remote(whole_c.at[me], whole_c.at[me], fc_ss.at[k], fc_rs.at[k], (px, py, z)).start()
    for k in order:
        total = grad_out[k, me].astype(F32)
        for j in range(1, parts):
            piece(k, j, me).wait()
            total = total + grad_in[k, j].astype(F32)
        piece_out[k] = total.astype(BF)
        if k > 0:
            remote(
                piece_out.at[k], whole_w.at[me, z], za_ss.at[k], za_rs.at[k], (ix, iy, af_peer(k))
            ).start()

    def share(k, j, slot, s, where):
        return remote(
            whole_w.at[slot, s], whole_w.at[slot, s], fw_ss.at[k, j], fw_rs.at[k, j], (*where, z)
        )

    whole_w[me, z] = piece_out[0]
    for k in range(af):
        here = lax.rem(z - k + af, af)
        if k > 0:
            remote(
                piece_out.at[k], whole_w.at[me, here], za_ss.at[k], za_rs.at[k], (ix, iy, here)
            ).wait_recv()
        for j in range(1, parts):
            share(k, j, me, here, plane_peer(j)).start()

    for k in range(1, af):
        remote(w_cols.at[z], w_cols.at[z], w_ss.at[k], w_rs.at[k], (ix, iy, af_peer(k))).wait_send()
        remote(
            grad_logits.at[z], grad_logits.at[z], gl_ss.at[k], gl_rs.at[k], (ix, iy, af_peer(k))
        ).wait_send()
        remote(piece_out.at[k], whole_w.at[me, z], za_ss.at[k], za_rs.at[k], (ix, iy, af_peer(k))).wait_send()
    for s in range(af):
        for c in range(CHUNKS):

            @pl.when(jnp.logical_and(s <= z, z + 1 < af))
            def _():
                up(s, c).wait_send()

            @pl.when(jnp.logical_and(s >= z, z > 0))
            def _():
                down(s, c).wait_send()

    for k in range(1, parts):
        px = lax.rem(ix - k // gy + gx, gx)
        py = lax.rem(iy - k % gy + gy, gy)
        slot = px * gy + py
        remote(whole_c.at[slot], whole_c.at[slot], fc_ss.at[k], fc_rs.at[k], (px, py, z)).wait()
        for m in range(af):
            share(m, k, slot, lax.rem(z - m + af, af), (px, py)).wait()
    out_c[...] = whole_c[...]
    for s in range(af):
        out_w[:, :, s * width : (s + 1) * width] = whole_w[:, s]


def local(
    sizes,
    features,
    adj_tiles,
    col_block,
    send_rows,
    send_counts,
    recv_target,
    edge_weight,
    labels,
    w_hidden,
    w_classes,
):
    gx, gy, af = sizes
    parts = gx * gy
    nodes, width = features.shape
    slots = send_rows.shape[1]
    classes = w_classes.shape[1]
    rows = width // parts
    vmem = pl.BlockSpec(memory_space=pltpu.VMEM)
    smem = pl.BlockSpec(memory_space=pltpu.SMEM)
    dma = pltpu.SemaphoreType.DMA
    grad_w, grad_c = pl.pallas_call(
        functools.partial(kernel, sizes),
        out_shape=(
            jax.ShapeDtypeStruct((parts, rows, af * width), BF),
            jax.ShapeDtypeStruct((parts, rows, classes), BF),
        ),
        in_specs=[vmem, vmem, vmem, vmem, smem, vmem, vmem, vmem, vmem, vmem],
        out_specs=(vmem, vmem),
        scratch_shapes=[
            pltpu.VMEM((4 * slots, nodes), BF),
            pltpu.VMEM((nodes, 4 * slots), BF),
            pltpu.VMEM((4 * slots, nodes), BF),
            pltpu.VMEM((nodes, 4 * slots), BF),
            pltpu.VMEM((slots, 8), F32),
            pltpu.VMEM((slots, 8), F32),
            pltpu.VMEM((nodes, nodes), BF),
            pltpu.VMEM((nodes, nodes), BF),
            pltpu.VMEM((nodes, width), F32),
            pltpu.VMEM((nodes, width), BF),
            pltpu.VMEM((3, 4, slots, width), BF),
            pltpu.VMEM((3, 4, slots, width), BF),
            pltpu.VMEM((4, slots, width), BF),
            pltpu.VMEM((af, nodes, width), BF),
            pltpu.VMEM((af, width, width), BF),
            pltpu.VMEM((nodes, width), F32),
            pltpu.VMEM((nodes, width), BF),
            pltpu.VMEM((af, nodes // af, classes), BF),
            pltpu.VMEM((af, nodes // af, classes), BF),
            pltpu.VMEM((af, nodes // af, classes), BF),
            pltpu.VMEM((af, parts, rows, width), BF),
            pltpu.VMEM((af, parts, rows, width), BF),
            pltpu.VMEM((parts, rows, classes), BF),
            pltpu.VMEM((parts, rows, classes), BF),
            pltpu.VMEM((af, rows, width), BF),
            pltpu.VMEM((parts, af, rows, width), BF),
            pltpu.VMEM((parts, rows, classes), BF),
            dma((3, 4)),
            dma((3, 4)),
            dma((af, CHUNKS)),
            dma((af, CHUNKS)),
            dma((af, CHUNKS)),
            dma((af,)),
            dma((af,)),
            dma((af,)),
            dma((af,)),
            dma((af,)),
            dma((af,)),
            dma((af, parts)),
            dma((af, parts)),
            dma((parts,)),
            dma((parts,)),
            dma((af,)),
            dma((af,)),
            dma((af, parts)),
            dma((af, parts)),
            dma((parts,)),
            dma((parts,)),
        ],
        compiler_params=pltpu.CompilerParams(
            collective_id=0, has_side_effects=True, vmem_limit_bytes=56 * 1024 * 1024
        ),
        name="gcn_step",
    )(
        features,
        adj_tiles,
        col_block,
        send_rows,
        send_counts,
        recv_target,
        edge_weight,
        labels.reshape(1, -1),
        w_hidden,
        w_classes,
    )
    return (
        grad_w.reshape(width, af * width).astype(F32),
        grad_c.reshape(width, classes).astype(F32),
    )


def solution(mesh):
    sizes = (mesh.shape["gx"], mesh.shape["gy"], mesh.shape["af"])
    placed = (
        P(("gx", "gy"), "af"),
        P(("gx", "gy"), None, None, None),
        P(("gx", "gy"), None),
        P(("gx", "gy"), None),
        P(("gx", "gy")),
        P(("gx", "gy"), None),
        P(("gx", "gy"), None),
        P(("gx", "gy")),
        P("af", None),
        P("af", None),
    )
    return jax.shard_map(
        functools.partial(local, sizes),
        mesh=mesh,
        in_specs=placed,
        out_specs=(P("af", None), P("af", None)),
        check_vma=False,
    )
```

time: 123 us -> 109 us (0.89)
  Pallas kernels: 111 us -> 104 us
  local copies, waits for them, and re-layouts: 6.82 us -> 1.35 us
    pallas_call x1, Pallas kernels: 111 us -> 104 us  [local(): pl.pallas_call(functools.partial(kernel, sizes), out_shape=(jax.ShapeDtyp...]
    unnamed x17 -> x3, local copies, waits for them, and re-layouts: 4.61 us -> 1.35 us
where the time goes in v2:
time: 109 us
  Pallas kernels  104 us (95%)
  other arithmetic  2.83 us (3%)
  local copies, waits for them, and re-layouts  1.35 us (1%)
    pallas_call x1, Pallas kernels, local(): pl.pallas_call(functools.partial(kernel, sizes), out_shape=(jax.ShapeDtyp...  104 us

profile of v2, /device:TPU:0, one launch (start us, length us, event | category | flops | bytes accessed | tf_op | source)
XLA Modules:
  0.0 109.3 jit_solution(4362687137706831921)
XLA Ops:
  0.6 1.3 %copy.12.colb = s32[8,4]{1,0:T(8,128)} copy(s32[8,4]{0,1:T(4,128)} %param.12) | data formatting | bytes 256 | tf_op args[2]
  2.0 104.5 %gcn_step.1 = (bf16[8,32,1024]{2,1,0:T(8,128)(2,1)}, bf16[8,32,128]{2,1,0:T(8,128)(2,1)}) custom-call(bf16[1024,256]{1,0:T(8,128)(2,1)} %feat.1, bf16[8,4,128,128]{3,2,1,0:T(8,128)(2,1)} %adj.1, s32[8,4]{1,0:T(8,128)} %copy.12.colb, s32[4,384]{1,0:T(4,128)} %send_rows.1, s32[4]{0:T(128)} %counts.1, s32[4,384]{1,0:T(4,128)} %recv_rows.1, f32[4,384]{1,0:T(4,128)} %weights.1, ...), custom_call_target="tpu_custom_call" | custom-call | tf_op jit(solution)/shard_map/gcn_step/pallas_call | solution.py:469
  106.4 0.0 copy-start
  106.5 2.2 %bitcast_convert_fusion = f32[256,1024]{1,0:T(8,128)} fusion(bf16[8,32,1024]{2,1,0:T(8,128)(2,1)} %get-tuple-element.4), kind=kLoop, calls=%fused_computation | loop fusion | flops 262144 | bytes 1572864 | tf_op jit(solution)/shard_map/convert_element_type | solution.py:544
  108.6 0.0 copy-done
  108.6 0.7 bitcast_convert_fusion.1
Async XLA Ops:
  106.4 2.2 %copy-start = (bf16[8,32,128]{2,1,0:T(8,128)(2,1)S(1)}, bf16[8,32,128]{2,1,0:T(8,128)(2,1)}, u32[]{:S(2)}) copy-start(bf16[8,32,128]{2,1,0:T(8,128)(2,1)} %get-tuple-element.5) | copy-start | bytes 196612

commit v3 on v2

--- a/solution.py
+++ b/solution.py
@@ -53,6 +53,7 @@
     halo_in,
     halo_low,
     gathered,
+    gathered_t,
     w_cols,
     pre,
     mixed_hidden,
@@ -228,16 +229,18 @@
 
     halo_send(0, feat, send_hot, False, ahead, ahead_id)
 
+    def gates(r, c):
+        lane_r = lax.broadcasted_iota(jnp.int32, (tiles, blocks), 1) == r
+        chosen = jnp.sum(jnp.where(lane_r, colb[...].astype(F32), 0.0), axis=1, keepdims=True)
+        return [jnp.where(chosen[k : k + 1, :] == c, 1.0, 0.0) for k in range(tiles)]
+
     @pl.loop(0, blocks)
     def _(r):
         values = [adj[r, k].astype(F32) for k in range(tiles)]
-        turned = [v.T for v in values]
-        chosen = colb[pl.ds(r, 1), :]
         across = pl.ds(pl.multiple_of(r * tb, tb), tb)
         for c in range(blocks):
-            gates = [jnp.where(chosen[:, k : k + 1] == c, 1.0, 0.0) for k in range(tiles)]
-            dense[across, c * tb : (c + 1) * tb] = sum(v * g for v, g in zip(values, gates)).astype(BF)
-            dense_t[c * tb : (c + 1) * tb, across] = sum(v * g for v, g in zip(turned, gates)).astype(BF)
+            tile = sum(v * g for v, g in zip(values, gates(r, c)))
+            dense[across, c * tb : (c + 1) * tb] = tile.astype(BF)
 
     local_part(dense, feat)
     build_cols(recv_hot_t, taken)
@@ -274,6 +277,15 @@
         at = slice(c * step, (c + 1) * step)
         pre[at, :] = mm(gathered[z, at], w_cols[z])
     build_cols(send_hot_t, live)
+
+    @pl.loop(0, blocks)
+    def _(r):
+        turned = [adj[r, k].astype(F32).T for k in range(tiles)]
+        across = pl.ds(pl.multiple_of(r * tb, tb), tb)
+        for c in range(blocks):
+            tile = sum(v * g for v, g in zip(turned, gates(r, c)))
+            dense_t[c * tb : (c + 1) * tb, across] = tile.astype(BF)
+
     build_rows(recv_hot, 4)
     for k in range(1, af):
         for c in range(CHUNKS):
@@ -307,6 +319,9 @@
 
     halo_send(1, field, send_hot, False, ahead, ahead_id)
     local_part(dense, field)
+    for s in range(af):
+        for i in range(nodes // 256):
+            gathered_t[s, :, i * 256 : (i + 1) * 256] = gathered[s, i * 256 : (i + 1) * 256].T
     own_logits = []
 
     def to_classes(add):
@@ -375,7 +390,7 @@
 
     order = (*range(1, af), 0)
     for k in order:
-        term = mm_tn(gathered[af_peer(k)], field[...])
+        term = mm(gathered_t[af_peer(k)], field[...])
         grad_out[k] = term.astype(BF).reshape(parts, rows, width)
         for j in range(1, parts):
             px, py = plane_peer(j)
@@ -489,6 +504,7 @@
             pltpu.VMEM((3, 4, slots, width), BF),
             pltpu.VMEM((4, slots, width), BF),
             pltpu.VMEM((af, nodes, width), BF),
+            pltpu.VMEM((af, width, nodes), BF),
             pltpu.VMEM((af, width, width), BF),
             pltpu.VMEM((nodes, width), F32),
             pltpu.VMEM((nodes, width), BF),
@@ -531,7 +547,7 @@
     )(
         features,
         adj_tiles,
-        col_block,
+        col_block.T,
         send_rows,
         send_counts,
         recv_target,

time: 109 us -> 109 us (level)
  Pallas kernels: 104 us -> 106 us
  local copies, waits for them, and re-layouts: 1.35 us -> 0.01 us
    unnamed x3 -> x2, local copies, waits for them, and re-layouts: 1.35 us -> 0.01 us
    pallas_call x1, Pallas kernels: 104 us -> 106 us  [local(): pl.pallas_call(functools.partial(kernel, sizes), out_shape=(jax.ShapeDtyp...]
where the time goes in v3:
time: 109 us
  Pallas kernels  106 us (97%)
  other arithmetic  2.83 us (3%)
    pallas_call x1, Pallas kernels, local(): pl.pallas_call(functools.partial(kernel, sizes), out_shape=(jax.ShapeDtyp...  106 us

profile of v3, /device:TPU:0, one launch (start us, length us, event | category | flops | bytes accessed | tf_op | source)
XLA Modules:
  0.0 109.1 jit_solution(3085598174263315561)
XLA Ops:
  0.6 105.6 %gcn_step.1 = (bf16[8,32,1024]{2,1,0:T(8,128)(2,1)}, bf16[8,32,128]{2,1,0:T(8,128)(2,1)}) custom-call(bf16[1024,256]{1,0:T(8,128)(2,1)} %feat.1, bf16[8,4,128,128]{3,2,1,0:T(8,128)(2,1)} %adj.1, s32[4,8]{1,0:T(4,128)} %bitcast.9, s32[4,384]{1,0:T(4,128)} %send_rows.1, s32[4]{0:T(128)} %counts.1, s32[4,384]{1,0:T(4,128)} %recv_rows.1, f32[4,384]{1,0:T(4,128)} %weights.1, ...), custom_call_target="tpu_custom_call" | custom-call | tf_op jit(solution)/shard_map/gcn_step/pallas_call | solution.py:484
  106.3 0.0 copy-start
  106.3 2.2 %bitcast_convert_fusion = f32[256,1024]{1,0:T(8,128)} fusion(bf16[8,32,1024]{2,1,0:T(8,128)(2,1)} %get-tuple-element.4), kind=kLoop, calls=%fused_computation | loop fusion | flops 262144 | bytes 1572864 | tf_op jit(solution)/shard_map/convert_element_type | solution.py:560
  108.4 0.0 copy-done
  108.4 0.7 bitcast_convert_fusion.1
Async XLA Ops:
  106.3 2.2 %copy-start = (bf16[8,32,128]{2,1,0:T(8,128)(2,1)S(1)}, bf16[8,32,128]{2,1,0:T(8,128)(2,1)}, u32[]{:S(2)}) copy-start(bf16[8,32,128]{2,1,0:T(8,128)(2,1)} %get-tuple-element.5) | copy-start | bytes 196612
